TPU v7x, 32 devices: a whole 2x2x4 slice. The times are simulated.
32 devices in a mesh: sens: 8 (over y, x, core), hour: 4 (over z).
Axes of the slice: x: 2, y: 2, z: 4, core: 2. Of those that a mesh axis runs over, the one named last changes fastest.
Arguments:
- sky: bfloat16 [512, 146], P('hour'), may hold values from 0.049804688 to 1
- sky_open: bfloat16 [146, 16384], P(None, 'sens'), may hold values from 0 to 0.013977051
- sky_closed: bfloat16 [146, 16384], P(None, 'sens'), may hold values from 0 to 0.0039978027
- sun_coef: bfloat16 [5165, 16384], P(None, ('sens', 'hour')), may hold values from 0 to 1
- sun_bins: int32 [512, 4], P('hour'), may hold values from 0 to 5164, as said below
- sun_rad: bfloat16 [512, 4], P('hour'), may hold values from 0.099609375 to 1
- target: bfloat16 [512, 16384], P('hour', 'sens'), may hold values from 0 to 2
- zone_of: int32 [8192, 1], P('sens'), may hold values from 0 to 7
- area: float32 [8192], P('sens'), may hold values from 0.5 to 4
- openness: float32 [8192], P('sens'), may hold values from 0 to 1
Outputs:
- illuminance: bfloat16 [512, 16384], P('hour', 'sens')
- new_openness: float32 [8192], P('sens')
Inputs may be any that keep to these rules, and one draw needn't show every extreme that they name: `sun_bins`: the 4 bins of one hour are consecutive modulo 5165, hence distinct. `zone_of`: every zone has at least one window.
All inputs are finite; a program needn't handle non-finite values.
Results may differ from a plain program's by a relative error of at most 0.001.
Values may be sent and summed in bfloat16 or wider, within the bound.
No kernel may reach another device: no remote copies, remote signals or barrier semaphores. Data moves between devices by JAX's collectives and lax.ppermute only.
A program may use at most 128 MiB of HBM per device.

v0:
```python
import jax
import jax.numpy as jnp
from jax import lax
from jax.sharding import PartitionSpec as P


def local(sky, sky_open, sky_closed, sun_coef, sun_bins, sun_rad, target, zone_of, area, openness):
    zone_count = lax.axis_size("sens")
    own_zone = lax.axis_index("sens")
    member = (zone_of[:, 0][:, None] == jnp.arange(zone_count, dtype=jnp.int32)[None, :]).astype(
        jnp.float32
    )
    stacked = jnp.stack([area * openness, area])
    partial_sums = jnp.dot(stacked, member, precision=lax.Precision.HIGHEST)
    totals = lax.psum(partial_sums, "sens")
    mine = lax.dynamic_slice_in_dim(totals, own_zone, 1, 1)[:, 0]
    share = mine[0] / mine[1]
    op_part = jnp.dot(sky, sky_open, preferred_element_type=jnp.float32)
    cl_part = jnp.dot(sky, sky_closed, preferred_element_type=jnp.float32)
    hour_rows = sky.shape[0]
    kbins = sun_bins.shape[1]
    nbins = sun_coef.shape[0]
    columns = jnp.arange(nbins, dtype=jnp.int32)[None, :]
    weights = jnp.zeros((hour_rows, nbins), jnp.float32)
    for slot in range(kbins):
        weights = weights + jnp.where(
            sun_bins[:, slot][:, None] == columns,
            sun_rad[:, slot][:, None].astype(jnp.float32),
            0.0,
        )
    weights = weights.astype(jnp.bfloat16)
    sun_part = jnp.dot(
        weights,
        lax.all_gather(sun_coef, "hour", axis=1, tiled=True),
        preferred_element_type=jnp.float32,
    )
    cross = op_part - cl_part + sun_part
    lit = cl_part + share * cross
    local_grad = jnp.sum(2.0 * (lit - target.astype(jnp.float32)) * cross)
    zone_grad = lax.psum(local_grad, "hour")
    ratio = zone_grad / mine[1]
    windows_all = area.shape[0] * zone_count
    ratio_all = lax.all_gather(ratio[None], "sens", axis=0, tiled=True)
    grad = area * jnp.dot(member, ratio_all, precision=lax.Precision.HIGHEST)
    square_sum = lax.psum(jnp.sum(grad * grad), "sens")
    rms = jnp.sqrt(square_sum / windows_all + 1e-06)
    new_openness = jnp.clip(openness - 0.25 * grad / rms, 0.0, 1.0)
    return (lit.astype(jnp.bfloat16), new_openness)


def solution(mesh):
    in_specs = (
        P("hour", None),
        P(None, "sens"),
        P(None, "sens"),
        P(None, ("sens", "hour")),
        P("hour", None),
        P("hour", None),
        P("hour", "sens"),
        P("sens", None),
        P("sens"),
        P("sens"),
    )
    out_specs = (P("hour", "sens"), P("sens"))
    return jax.shard_map(local, mesh=mesh, in_specs=in_specs, out_specs=out_specs, check_vma=False)
```

profile of v0, /device:TPU:0, one launch (start us, length us, event | category | flops | bytes accessed | tf_op | source)
XLA Modules:
  0.0 430.9 jit_solution(12331731021801923692)
XLA Ops:
  7.2 0.0 copy-start
  7.2 0.0 copy-start.9
  7.3 0.0 all-gather.2.cloned.1.call-start
  7.3 0.7 all-gather.2.cloned.1.call-update
  8.0 0.0 copy-done.4
  8.0 0.0 copy-done.5
  8.0 0.7 fusion.13
  8.7 15.1 %psum.21 = f32[2,8]{0,1:T(8,128)S(1)} all-reduce(f32[2,8]{0,1:T(8,128)S(1)} %fusion.13), channel_id=1, replica_groups=mesh['sens'=8,'hour'=4] {'sens'}, use_global_device_ids=true, to_apply=%region_0.0 | all-reduce | flops 16 | bytes 128 | tf_op jit(solution)/shard_map/psum | solution.py:15
  23.9 0.6 fusion.22
  25.8 0.7 dynamic-slice
  26.5 0.0 copy-done.6
  26.5 0.0 copy-done.7
  26.5 0.3 fusion.23
  26.9 345.6 %all-gather.2.cloned.1.call-done = bf16[5165,2048]{1,0:T(8,128)(2,1)} async-done(((bf16[5165,512]{1,0:T(8,128)(2,1)}), bf16[5165,2048]{1,0:T(8,128)(2,1)}) %all-gather.2.cloned.1.call-update) | async-done | bytes 21155856 | tf_op jit(solution)/shard_map/all_gather | solution.py:34
  372.5 11.0 %fusion.1 = f32[128,2048]{1,0:T(8,128)S(1)} fusion(bf16[5165,2048]{1,0:T(8,128)(2,1)} %all-gather.2.cloned.1.call-done, f32[128]{0:T(128)S(1)} %get-tuple-element.10, s32[128]{0:T(128)S(1)} %get-tuple-element.6, f32[128]{0:T(128)S(1)} %get-tuple-element.11, s32[128]{0:T(128)S(1)} %get-tuple-element.7, f32[128]{0:T(128)S(1)} %get-tuple-element.9, ...), kind=kOutput, calls=%fused_computation.7 | convolution fusion | flops 2715880960 | bytes 22208512 | tf_op jit(solution)/shard_map/dot_general | solution.py:32
  383.5 0.0 copy-done
  383.5 2.0 multiply_reduce_fusion
  385.5 9.6 %psum.22 = f32[]{:T(128)} all-reduce(f32[]{:T(128)} %get-tuple-element.2), channel_id=1, replica_groups=mesh['sens'=8,'hour'=4] {'hour'}, use_global_device_ids=true, to_apply=%region_2.3 | all-reduce | flops 1 | bytes 8 | tf_op jit(solution)/shard_map/psum | solution.py:40
  396.4 0.8 dynamic-update-slice
  397.2 12.0 %all-reduce = f32[8]{0:T(128)S(1)} all-reduce(f32[8]{0:T(128)S(1)} %dynamic-update-slice), channel_id=1, replica_groups=mesh['sens'=8,'hour'=4] {'sens'}, use_global_device_ids=true, to_apply=%add | all-reduce | flops 8 | bytes 64
  409.2 0.4 fusion.12
  409.7 0.6 multiply_reduce_fusion.1
  410.3 12.4 %psum.23 = f32[]{:T(128)} all-reduce(f32[]{:T(128)} %multiply_reduce_fusion.1), channel_id=1, replica_groups=mesh['sens'=8,'hour'=4] {'sens'}, use_global_device_ids=true, to_apply=%region_4.5 | all-reduce | flops 1 | bytes 8 | tf_op jit(solution)/shard_map/psum | solution.py:45
  423.4 0.6 subtract_clamp_fusion
  (18 shorter events, 0.1 us)
Async XLA Ops:
  7.2 376.3 %copy-start = (bf16[146,2048]{1,0:T(8,128)(2,1)S(1)}, bf16[146,2048]{1,0:T(8,128)(2,1)}, u32[]{:S(2)}) copy-start(bf16[146,2048]{1,0:T(8,128)(2,1)} %param.11) | copy-start | bytes 1794052
  7.2 18.6 %copy-start.9 = (u32[32]{0:T(128)S(1)}, u32[32]{0:T(128)}, u32[]{:S(2)}) copy-start(u32[32]{0:T(128)} %constant.25) | copy-start | bytes 388
  7.2 0.8 copy-start.4
  7.2 0.8 copy-start.5
  7.2 0.8 copy-start.8
  7.2 19.3 %copy-start.6 = (bf16[128,4]{0,1:T(4,128)(2,1)S(1)}, bf16[128,4]{0,1:T(4,128)(2,1)}, u32[]{:S(2)}) copy-start(bf16[128,4]{0,1:T(4,128)(2,1)} %param.15) | copy-start | bytes 3076
  7.2 19.3 %copy-start.7 = (s32[128,4]{0,1:T(4,128)S(1)}, s32[128,4]{0,1:T(4,128)}, u32[]{:S(2)}) copy-start(s32[128,4]{0,1:T(4,128)} %param.14) | copy-start | bytes 6148
  7.2 19.3 %copy-start.3 = (bf16[128,146]{0,1:T(8,128)(2,1)S(1)}, bf16[128,146]{0,1:T(8,128)(2,1)}, u32[]{:S(2)}) copy-start(bf16[128,146]{0,1:T(8,128)(2,1)} %param.10) | copy-start | bytes 112132
  7.3 19.3 %copy-start.1 = (bf16[146,2048]{1,0:T(8,128)(2,1)S(1)}, bf16[146,2048]{1,0:T(8,128)(2,1)}, u32[]{:S(2)}) copy-start(bf16[146,2048]{1,0:T(8,128)(2,1)} %param.12) | copy-start | bytes 1794052
  7.3 365.2 %all-gather.2.cloned.1.call-start = ((), (), s32[]{:S(2)}) async-start(), calls=%async_computation | async-start | bytes 26460160 | tf_op jit(solution)/shard_map/all_gather | solution.py:34
  372.5 11.0 %copy-start.2 = (bf16[128,2048]{1,0:T(8,128)(2,1)S(1)}, bf16[128,2048]{1,0:T(8,128)(2,1)}, u32[]{:S(2)}) copy-start(bf16[128,2048]{1,0:T(8,128)(2,1)} %param.16) | copy-start | bytes 1572868
Sparse Core Ops, SparseCore 0:
  9.7 362.7 all-gather.1
where the time goes:
time: 431 us
  waiting for transfers between devices  346 us (80%)
  blocking collectives  49.2 us (11%)
  between operations  17.5 us (4%)
  matrix products  14.5 us (3%)
    all_gather x1, waiting for transfers between devices, local(): lax.all_gather(sun_coef, 'hour', axis=1, tiled=True)  346 us
    psum x1, blocking collectives, local(): totals = lax.psum(partial_sums, 'sens')  15.1 us
    psum x1, blocking collectives, local(): square_sum = lax.psum(jnp.sum(grad * grad), 'sens')  12.4 us
    unnamed x1, blocking collectives  12 us
    dot_general x1, matrix products, local(): jnp.dot(weights, lax.all_gather(sun_coef, 'hour', axis=1, tiled=True), pr...  11 us
    psum x1, blocking collectives, local(): zone_grad = lax.psum(local_grad, 'hour')  9.57 us
  transfers between devices with their start and end apart: 1, of which 1 were waited for; matrix products, arithmetic and copies ran while one was open for 1% of the time, Pallas kernels for 0%

commit v1 on v0

v1 whole, which is shorter than its diff:
```python
import jax
import jax.numpy as jnp
from jax import lax
from jax.experimental import pallas as pl
from jax.experimental.pallas import tpu as pltpu
from jax.sharding import PartitionSpec as P

LANES = 128
CHUNK = 1024
HEAD = 16
VMEM_BYTES = 32 * 1024 * 1024


def call(kernel, name, out_shape, flops=0, moved=0, **more):
    return pl.pallas_call(
        kernel,
        out_shape=out_shape,
        name=name,
        compiler_params=pltpu.CompilerParams(vmem_limit_bytes=VMEM_BYTES),
        cost_estimate=pl.CostEstimate(flops=flops, bytes_accessed=moved, transcendentals=0),
        **more,
    )


def pack_kernel(sky_ref, bins_ref, rad_ref, out_ref):
    bins = bins_ref[:]
    kbins = bins.shape[0]
    fill = jnp.zeros((HEAD - 3 * kbins, bins.shape[1]), jnp.float32)
    parts = [rad_ref[:].astype(jnp.float32), (bins // LANES).astype(jnp.float32), (bins % LANES).astype(jnp.float32)]
    head = jnp.concatenate(parts + [fill], axis=0).astype(jnp.bfloat16)
    for g in range(out_ref.shape[0]):
        out_ref[g, :HEAD] = head
        out_ref[g, HEAD:] = sky_ref[:]


def sums_kernel(zone_ref, area_ref, openness_ref, target_ref, sums_ref, split_ref):
    zone, area = zone_ref[:], area_ref[:]
    lane = lax.broadcasted_iota(jnp.int32, (1, LANES), 1)
    values = [area * openness_ref[:], area, area * area]
    for z in range(sums_ref.shape[0]):
        member = zone == z
        row = jnp.zeros((1, LANES), jnp.float32)
        for k, value in enumerate(values):
            row = jnp.where(lane == k, jnp.sum(jnp.where(member, value, 0.0), keepdims=True), row)
        sums_ref[z] = row
    width = split_ref.shape[2]
    for g in range(split_ref.shape[0]):
        split_ref[g] = target_ref[:, g * width : (g + 1) * width]


def lit_kernel(nbins, chunks, groups, kbins, patches):
    def kernel(place_ref, sums_ref, packed, open_ref, closed_ref, coef_ref, lits, cross_ref, own_ref, acc, pattern, block):
        rows = packed.shape[2]
        step = pl.program_id(0)

        @pl.when(step == 0)
        def _():
            lane = lax.broadcasted_iota(jnp.int32, (rows, LANES), 1)
            for g in range(groups):
                small = packed[g, :HEAD].astype(jnp.float32).T
                value = jnp.zeros((rows, LANES), jnp.float32)
                where = jnp.zeros((rows, LANES), jnp.float32)
                for k in range(kbins):
                    low = small[:, 2 * kbins + k : 2 * kbins + k + 1].astype(jnp.int32)
                    hit = lane == low
                    value = jnp.where(hit, small[:, k : k + 1], value)
                    where = jnp.where(hit, small[:, kbins + k : kbins + k + 1], where)
                pattern[g * rows : (g + 1) * rows] = value
                block[g * rows : (g + 1) * rows] = where

        def weights(first, count):
            parts = []
            for c in range(count):
                here = block[:] == (first + c).astype(jnp.float32)
                parts.append(jnp.where(here, pattern[:], 0.0).astype(jnp.bfloat16))
            return jnp.concatenate(parts, axis=1) if count > 1 else parts[0]

        per = CHUNK // LANES
        last = nbins - (chunks - 1) * CHUNK
        last_parts = pl.cdiv(last, LANES)

        @pl.when(step < chunks - 1)
        def _():
            part = jnp.dot(weights(step * per, per), coef_ref[:], preferred_element_type=jnp.float32)

            @pl.when(step == 0)
            def _():
                acc[:] = part

            @pl.when(step > 0)
            def _():
                acc[:] = acc[:] + part

        @pl.when(step == chunks - 1)
        def _():
            tail = coef_ref[: last_parts * LANES]
            row = lax.broadcasted_iota(jnp.int32, tail.shape, 0)
            tail = jnp.where(row < last, tail, jnp.zeros_like(tail))
            part = jnp.dot(weights(step * per, last_parts), tail, preferred_element_type=jnp.float32)
            mine = jnp.sum(sums_ref[:], axis=0)
            share = mine[:, 0:1] / mine[:, 1:2]
            total = jnp.zeros((8, acc.shape[1]), jnp.float32)
            for g in range(groups):
                sky = packed[g, HEAD:]
                at = slice(g * rows, (g + 1) * rows)
                over = (((0,), (0,)), ((), ()))
                op = lax.dot_general(sky, open_ref[:], over, preferred_element_type=jnp.float32)
                cl = lax.dot_general(sky, closed_ref[:], over, preferred_element_type=jnp.float32)
                cross = op - cl + (acc[at] + part[at])
                lit = cl + share * cross
                lits[g] = lit.astype(jnp.bfloat16)
                cross_ref[at] = cross
                total = total + jnp.sum((lit * cross).reshape(rows // 8, 8, -1), axis=0)
            own_ref[:] = total

    return kernel


def grad_kernel(sums_ref, own_ref, cross_ref, targets, out_ref):
    groups, rows, _ = targets.shape
    total = own_ref[:]
    for g in range(groups):
        term = targets[g].astype(jnp.float32) * cross_ref[g * rows : (g + 1) * rows]
        total = total - jnp.sum(term.reshape(rows // 8, 8, -1), axis=0)
    mine = jnp.sum(sums_ref[:], axis=0)
    lane = lax.broadcasted_iota(jnp.int32, (1, LANES), 1)
    ratio = 2.0 * jnp.sum(total, keepdims=True) / mine[:, 1:2]
    row = jnp.where(lane == 0, ratio, jnp.where(lane == 1, mine[:, 2:3], 0.0))
    out_ref[:] = jnp.broadcast_to(row[None], out_ref.shape)


def step_kernel(groups, windows):
    def kernel(heard_ref, zone_ref, area_ref, openness_ref, out_ref):
        zone = zone_ref[:]
        chosen = jnp.zeros(zone.shape, jnp.float32)
        square = jnp.zeros((1, 1), jnp.float32)
        for z in range(heard_ref.shape[0] // groups):
            heard = heard_ref[z * groups : (z + 1) * groups]
            ratio = jnp.sum(heard, axis=0)[:, 0:1]
            square = square + ratio * ratio * heard[0, :, 1:2]
            chosen = jnp.where(zone == z, ratio, chosen)
        rms = jnp.sqrt(square / windows + 1e-06)
        out_ref[:] = jnp.clip(openness_ref[:] - 0.25 * (area_ref[:] * chosen) / rms, 0.0, 1.0)

    return kernel


def place_kernel(blocks, out_ref):
    width = blocks.shape[2]
    for g in range(blocks.shape[0]):
        out_ref[:, g * width : (g + 1) * width] = blocks[g]


def local(sky, sky_open, sky_closed, sun_coef, sun_bins, sun_rad, target, zone_of, area, openness):
    zones = lax.axis_size("sens")
    groups = lax.axis_size("hour")
    own_hour = lax.axis_index("hour").astype(jnp.int32)
    rows, patches = sky.shape
    kbins = sun_bins.shape[1]
    nbins, width = sun_coef.shape
    hours = rows * groups
    windows = area.shape[0]
    assert nbins % LANES == 0 or nbins % LANES >= 2 * kbins
    assert nbins <= 256 * LANES and width % LANES == 0 and windows % LANES == 0 and 3 * kbins <= HEAD
    shape = jax.ShapeDtypeStruct
    f32, bf16 = jnp.float32, jnp.bfloat16

    packed = call(pack_kernel, "pack", shape((groups, HEAD + patches, rows), bf16))(sky.T, sun_bins.T, sun_rad.T)
    packs = lax.all_to_all(packed, "hour", 0, 0)

    tiles = (windows // LANES, LANES)
    zone2, area2, openness2 = zone_of.reshape(tiles), area.reshape(tiles), openness.reshape(tiles)
    zone_sums, split = call(
        sums_kernel,
        "sums",
        [shape((zones, 1, LANES), f32), shape((groups, rows, width), bf16)],
        moved=4 * hours * width,
    )(zone2, area2, openness2, target)
    mine = lax.all_to_all(zone_sums, "sens", 0, 0)
    targets = lax.all_to_all(split, "hour", 0, 0)

    chunks = pl.cdiv(nbins, CHUNK)
    whole = lambda dims: pl.BlockSpec(dims, lambda i, place: (0,) * len(dims))
    column = pl.BlockSpec((patches, width), lambda i, place: (0, place[0]))
    lits, cross, own_sum = call(
        lit_kernel(nbins, chunks, groups, kbins, patches),
        "lit",
        [shape((groups, rows, width), bf16), shape((hours, width), f32), shape((8, width), f32)],
        flops=2 * hours * (nbins + 2 * patches) * width,
        moved=2 * nbins * width,
        grid_spec=pltpu.PrefetchScalarGridSpec(
            num_scalar_prefetch=1,
            grid=(chunks,),
            in_specs=[whole(mine.shape), whole(packs.shape), column, column]
            + [pl.BlockSpec((CHUNK, width), lambda i, place: (i, 0))],
            out_specs=[whole((groups, rows, width)), whole((hours, width)), whole((8, width))],
            scratch_shapes=[
                pltpu.VMEM((hours, width), f32),
                pltpu.VMEM((hours, LANES), f32),
                pltpu.VMEM((hours, LANES), f32),
            ],
        ),
    )(own_hour[None], mine, packs, sky_open, sky_closed, sun_coef)
    placed = lax.all_to_all(lits, "hour", 0, 0)

    message = call(
        grad_kernel,
        "grad",
        shape((zones * groups, 1, LANES), f32),
        flops=2 * hours * width,
        moved=6 * hours * width,
    )(mine, own_sum, cross, targets)
    heard = lax.all_to_all(message, ("sens", "hour"), 0, 0)
    new_openness = call(step_kernel(groups, windows * zones), "step", shape(tiles, f32))(heard, zone2, area2, openness2)
    illuminance = call(place_kernel, "place", shape((rows, groups * width), bf16), moved=4 * hours * width)(placed)
    return (illuminance, new_openness.reshape(-1))


def solution(mesh):
    in_specs = (
        P("hour", None),
        P(None, "sens"),
        P(None, "sens"),
        P(None, ("sens", "hour")),
        P("hour", None),
        P("hour", None),
        P("hour", "sens"),
        P("sens", None),
        P("sens"),
        P("sens"),
    )
    out_specs = (P("hour", "sens"), P("sens"))
    return jax.shard_map(local, mesh=mesh, in_specs=in_specs, out_specs=out_specs, check_vma=False)
```

time: 431 us -> 72.1 us (0.17)
  waiting for transfers between devices: 346 us -> 18.2 us
  blocking collectives: 49.2 us -> 21.3 us
  between operations: 17.5 us -> 0.71 us
  matrix products: 14.5 us -> 0 us
  starting transfers between devices: 0.04 us -> 12.1 us
  Pallas kernels: 0 us -> 9.26 us
  local copies, waits for them, and re-layouts: 2.12 us -> 9.88 us
    all_gather x1 -> x0, waiting for transfers between devices: 346 us -> none  [local(): lax.all_gather(sun_coef, 'hour', axis=1, tiled=True)]
    psum x3 -> x0, blocking collectives: 37.1 us -> none  [the longest x1 15.1 us: local(): totals = lax.psum(partial_sums, 'sens')]
    all_to_all x0 -> x2, blocking collectives: none -> 21.3 us  [the longest x1 11.7 us: local(): packs = lax.all_to_all(packed, 'hour', 0, 0)]
    all_to_all x0 -> x3, waiting for transfers between devices: none -> 18.2 us  [the longest x1 13.9 us: local(): placed = lax.all_to_all(lits, 'hour', 0, 0)]
    dot_general x5 -> x0, matrix products: 14.5 us -> none  [the longest x1 11 us: local(): jnp.dot(weights, lax.all_gather(sun_coef, 'hour', axis=1, tiled=True), pr...]
    all_to_all x0 -> x3, starting transfers between devices: none -> 12.1 us  [the longest x1 5.17 us: local(): mine = lax.all_to_all(zone_sums, 'sens', 0, 0)]
    unnamed x1 -> x0, blocking collectives: 12 us -> none
    pallas_call x0 -> x6, Pallas kernels: none -> 9.26 us  [the longest x1 6.47 us: local(): call(lit_kernel(nbins, chunks, groups, kbins, patches), 'lit', [shape((gr...]
  transfers between devices with their start and end apart: 1 -> 3, of which waited for: 1 -> 3; matrix products, arithmetic and copies ran while one was open for 1% -> 0% of each run, Pallas kernels for 0% -> 10%
where the time goes in v1:
time: 72.1 us; the launch traced here: 71.4 us
  blocking collectives  21.3 us (30%)
  waiting for transfers between devices  18.2 us (25%)
  starting transfers between devices  12.1 us (17%)
  local copies, waits for them, and re-layouts  9.88 us (14%)
  Pallas kernels  9.26 us (13%)
    all_to_all x1, waiting for transfers between devices, local(): placed = lax.all_to_all(lits, 'hour', 0, 0)  13.9 us
    all_to_all x1, blocking collectives, local(): packs = lax.all_to_all(packed, 'hour', 0, 0)  11.7 us
    unnamed x26, local copies, waits for them, and re-layouts  9.88 us
    all_to_all x1, blocking collectives, local(): heard = lax.all_to_all(message, ('sens', 'hour'), 0, 0)  9.52 us
    pallas_call x1, Pallas kernels, local(): call(lit_kernel(nbins, chunks, groups, kbins, patches), 'lit', [shape((gr...  6.47 us
    all_to_all x1, starting transfers between devices, local(): mine = lax.all_to_all(zone_sums, 'sens', 0, 0)  5.17 us
    all_to_all x1, starting transfers between devices, local(): targets = lax.all_to_all(split, 'hour', 0, 0)  3.47 us
    all_to_all x1, starting transfers between devices, local(): placed = lax.all_to_all(lits, 'hour', 0, 0)  3.47 us
  transfers between devices with their start and end apart: 3, of which 3 were waited for; matrix products, arithmetic and copies ran while one was open for 0% of the time, Pallas kernels for 10%

profile of v1, /device:TPU:0, one launch (start us, length us, event | category | flops | bytes accessed | tf_op | source)
XLA Modules:
  0.0 71.4 jit_solution(17681802642943975332)
XLA Ops:
  0.6 1.0 %copy-done = bf16[128,2048]{1,0:T(8,128)(2,1)S(1)} copy-done((bf16[128,2048]{1,0:T(8,128)(2,1)S(1)}, bf16[128,2048]{1,0:T(8,128)(2,1)}, u32[]{:S(2)}) %copy-start) | copy-done | bytes 524312
  1.7 0.7 copy-done.2
  2.4 0.7 copy-done.4
  3.0 0.7 copy-done.6
  3.7 0.9 %sums.1 = (f32[8,1,128]{2,1,0:T(1,128)}, bf16[4,128,512]{2,1,0:T(8,128)(2,1)}) custom-call(s32[8,128]{1,0:T(8,128)S(1)} %bitcast.9, f32[8,128]{1,0:T(8,128)S(1)} %bitcast.11, f32[8,128]{1,0:T(8,128)S(1)} %bitcast.13, bf16[128,2048]{1,0:T(8,128)(2,1)S(1)} %copy-done), custom_call_target="tpu_custom_call" | custom-call | bytes 1048576 | tf_op jit(solution)/shard_map/sums/pallas_call | solution.py:173
  4.6 5.2 %all-to-all-start = ((f32[8,1,128]{2,1,0:T(1,128)}), f32[8,1,128]{2,1,0:T(1,128)S(1)}, u32[]{:S(2)}, u32[]{:S(2)}) async-start(f32[8,1,128]{2,1,0:T(1,128)} %get-tuple-element.7), calls=%async_computation | async-start | bytes 8192 | tf_op jit(solution)/shard_map/all_to_all | solution.py:179
  9.8 0.8 %copy-done.1 = bf16[128,146]{0,1:T(8,128)(2,1)S(1)} copy-done((bf16[128,146]{0,1:T(8,128)(2,1)S(1)}, bf16[128,146]{0,1:T(8,128)(2,1)}, u32[]{:S(2)}) %copy-start.1) | copy-done | bytes 37400
  10.6 0.7 copy-done.8
  11.2 0.7 copy-done.9
  12.0 2.4 %all-to-all-done.sums_ref = f32[8,1,128]{2,1,0:T(1,128)S(1)} async-done(((f32[8,1,128]{2,1,0:T(1,128)}), f32[8,1,128]{2,1,0:T(1,128)S(1)}, u32[]{:S(2)}, u32[]{:S(2)}) %all-to-all-start) | async-done | bytes 4128 | tf_op jit(solution)/shard_map/all_to_all | solution.py:179
  14.4 11.7 %all_to_all.25.packed = bf16[4,162,128]{2,1,0:T(8,128)(2,1)S(1)} all-to-all(bf16[4,162,128]{2,1,0:T(8,128)(2,1)S(1)} %pack.1), channel_id=1, replica_groups=mesh['sens'=8,'hour'=4] {'hour'}, dimensions={0} | all-to-all | bytes 331776 | tf_op jit(solution)/shard_map/all_to_all | solution.py:169
  26.1 3.5 %all-to-all-start.3 = ((bf16[4,128,512]{2,1,0:T(8,128)(2,1)}), bf16[4,128,512]{2,1,0:T(8,128)(2,1)S(1)}, u32[]{:S(2)}, u32[]{:S(2)}) async-start(bf16[4,128,512]{2,1,0:T(8,128)(2,1)} %get-tuple-element.11), calls=%async_computation.3 | async-start | bytes 1048576 | tf_op jit(solution)/shard_map/all_to_all | solution.py:180
  29.6 0.0 copy-start.10
  29.6 2.5 %copy-done.10 = bf16[5165,512]{1,0:T(8,128)(2,1)S(1)} copy-done((bf16[5165,512]{1,0:T(8,128)(2,1)S(1)}, bf16[5165,512]{1,0:T(8,128)(2,1)}, u32[]{:S(2)}) %copy-start.10) | copy-done | bytes 5288984
  32.1 1.1 %copy-done.11 = bf16[146,2048]{1,0:T(8,128)(2,1)S(1)} copy-done((bf16[146,2048]{1,0:T(8,128)(2,1)S(1)}, bf16[146,2048]{1,0:T(8,128)(2,1)}, u32[]{:S(2)}) %copy-start.11) | copy-done | bytes 598040
  33.2 1.1 %copy-done.12 = bf16[146,2048]{1,0:T(8,128)(2,1)S(1)} copy-done((bf16[146,2048]{1,0:T(8,128)(2,1)S(1)}, bf16[146,2048]{1,0:T(8,128)(2,1)}, u32[]{:S(2)}) %copy-start.12) | copy-done | bytes 598040
  34.3 6.5 %lit.1 = (bf16[4,128,512]{2,1,0:T(8,128)(2,1)}, f32[512,512]{1,0:T(8,128)S(1)}, f32[8,512]{1,0:T(8,128)S(1)}) custom-call(s32[1]{0:T(128)} %bitcast.place_ref, f32[8,1,128]{2,1,0:T(1,128)S(1)} %all-to-all-done.sums_ref, bf16[4,162,128]{2,1,0:T(8,128)(2,1)S(1)} %all_to_all.25.packed, bf16[146,2048]{1,0:T(8,128)(2,1)S(1)} %copy-done.11, ...), custom_call_target="tpu_custom_call" | custom-call | flops 2861039616 | bytes 5288960 | tf_op jit(solution)/shard_map/lit/pallas_call | solution.py:185
  40.7 1.8 %all-to-all-done.3.targets = bf16[4,128,512]{2,1,0:T(8,128)(2,1)S(1)} async-done(((bf16[4,128,512]{2,1,0:T(8,128)(2,1)}), bf16[4,128,512]{2,1,0:T(8,128)(2,1)S(1)}, u32[]{:S(2)}, u32[]{:S(2)}) %all-to-all-start.3) | async-done | bytes 524320 | tf_op jit(solution)/shard_map/all_to_all | solution.py:180
  42.6 0.3 grad.1
  42.9 9.5 %all_to_all.26.heard_ref = f32[32,1,128]{2,1,0:T(1,128)S(1)} all-to-all(f32[32,1,128]{2,1,0:T(1,128)S(1)} %grad.1), channel_id=1, replica_groups=mesh['sens'=8,'hour'=4] {'sens','hour'}, dimensions={0} | all-to-all | bytes 32768 | tf_op jit(solution)/shard_map/all_to_all | solution.py:213
  52.4 3.5 %all-to-all-start.2 = ((bf16[4,128,512]{2,1,0:T(8,128)(2,1)}), bf16[4,128,512]{2,1,0:T(8,128)(2,1)S(1)}, u32[]{:S(2)}, u32[]{:S(2)}) async-start(bf16[4,128,512]{2,1,0:T(8,128)(2,1)} %get-tuple-element.8), calls=%async_computation.2 | async-start | bytes 1048576 | tf_op jit(solution)/shard_map/all_to_all | solution.py:204
  55.9 0.7 %step.1 = f32[8,128]{1,0:T(8,128)} custom-call(f32[32,1,128]{2,1,0:T(1,128)S(1)} %all_to_all.26.heard_ref, s32[8,128]{1,0:T(8,128)S(1)} %bitcast.10, f32[8,128]{1,0:T(8,128)S(1)} %bitcast.12, f32[8,128]{1,0:T(8,128)S(1)} %bitcast.14), custom_call_target="tpu_custom_call" | custom-call | tf_op jit(solution)/shard_map/step/pallas_call | solution.py:214
  56.7 13.9 %all-to-all-done.2.blocks = bf16[4,128,512]{2,1,0:T(8,128)(2,1)S(1)} async-done(((bf16[4,128,512]{2,1,0:T(8,128)(2,1)}), bf16[4,128,512]{2,1,0:T(8,128)(2,1)S(1)}, u32[]{:S(2)}, u32[]{:S(2)}) %all-to-all-start.2) | async-done | bytes 524320 | tf_op jit(solution)/shard_map/all_to_all | solution.py:204
  70.6 0.8 %place.1 = bf16[128,2048]{1,0:T(8,128)(2,1)} custom-call(bf16[4,128,512]{2,1,0:T(8,128)(2,1)S(1)} %all-to-all-done.2.blocks), custom_call_target="tpu_custom_call" | custom-call | bytes 1048576 | tf_op jit(solution)/shard_map/place/pallas_call | solution.py:215
  (16 shorter events, 0.0 us)
Async XLA Ops:
  0.6 1.0 %copy-start = (bf16[128,2048]{1,0:T(8,128)(2,1)S(1)}, bf16[128,2048]{1,0:T(8,128)(2,1)}, u32[]{:S(2)}) copy-start(bf16[128,2048]{1,0:T(8,128)(2,1)} %target_ref.1) | copy-start | bytes 1572868
  1.7 0.7 copy-start.2
  2.4 0.7 copy-start.4
  3.0 0.7 copy-start.6
  4.6 9.8 %all-to-all-start = ((f32[8,1,128]{2,1,0:T(1,128)}), f32[8,1,128]{2,1,0:T(1,128)S(1)}, u32[]{:S(2)}, u32[]{:S(2)}) async-start(f32[8,1,128]{2,1,0:T(1,128)} %get-tuple-element.7), calls=%async_computation | async-start | bytes 8192 | tf_op jit(solution)/shard_map/all_to_all | solution.py:179
  9.8 0.8 %copy-start.1 = (bf16[128,146]{0,1:T(8,128)(2,1)S(1)}, bf16[128,146]{0,1:T(8,128)(2,1)}, u32[]{:S(2)}) copy-start(bf16[128,146]{0,1:T(8,128)(2,1)} %param.10) | copy-start | bytes 112132
  10.6 0.7 copy-start.8
  11.2 0.7 copy-start.9
  26.1 16.5 %all-to-all-start.3 = ((bf16[4,128,512]{2,1,0:T(8,128)(2,1)}), bf16[4,128,512]{2,1,0:T(8,128)(2,1)S(1)}, u32[]{:S(2)}, u32[]{:S(2)}) async-start(bf16[4,128,512]{2,1,0:T(8,128)(2,1)} %get-tuple-element.11), calls=%async_computation.3 | async-start | bytes 1048576 | tf_op jit(solution)/shard_map/all_to_all | solution.py:180
  29.6 2.5 %copy-start.10 = (bf16[5165,512]{1,0:T(8,128)(2,1)S(1)}, bf16[5165,512]{1,0:T(8,128)(2,1)}, u32[]{:S(2)}) copy-start(bf16[5165,512]{1,0:T(8,128)(2,1)} %coef_ref.1) | copy-start | bytes 15866884
  32.1 1.1 %copy-start.11 = (bf16[146,2048]{1,0:T(8,128)(2,1)S(1)}, bf16[146,2048]{1,0:T(8,128)(2,1)}, u32[]{:S(2)}) copy-start(bf16[146,2048]{1,0:T(8,128)(2,1)} %open_ref.1) | copy-start | bytes 1794052
  33.2 1.1 %copy-start.12 = (bf16[146,2048]{1,0:T(8,128)(2,1)S(1)}, bf16[146,2048]{1,0:T(8,128)(2,1)}, u32[]{:S(2)}) copy-start(bf16[146,2048]{1,0:T(8,128)(2,1)} %closed_ref.1) | copy-start | bytes 1794052
  34.3 21.6 %copy-start.3 = (s32[1024,1]{0,1:T(1,128)S(1)}, s32[1024,1]{0,1:T(1,128)}, u32[]{:S(2)}) copy-start(s32[1024,1]{0,1:T(1,128)} %param.17) | copy-start | bytes 12292
  34.3 21.6 %copy-start.5 = (f32[1024]{0:T(1024)S(1)}, f32[1024]{0:T(1024)}, u32[]{:S(2)}) copy-start(f32[1024]{0:T(1024)} %param.18) | copy-start | bytes 12292
  34.3 21.7 %copy-start.7 = (f32[1024]{0:T(1024)S(1)}, f32[1024]{0:T(1024)}, u32[]{:S(2)}) copy-start(f32[1024]{0:T(1024)} %param.19) | copy-start | bytes 12292
  52.4 18.1 %all-to-all-start.2 = ((bf16[4,128,512]{2,1,0:T(8,128)(2,1)}), bf16[4,128,512]{2,1,0:T(8,128)(2,1)S(1)}, u32[]{:S(2)}, u32[]{:S(2)}) async-start(bf16[4,128,512]{2,1,0:T(8,128)(2,1)} %get-tuple-element.8), calls=%async_computation.2 | async-start | bytes 1048576 | tf_op jit(solution)/shard_map/all_to_all | solution.py:204

commit v2 on v0

v2 whole, which is shorter than its diff:
```python
import jax
import jax.numpy as jnp
from jax import lax
from jax.experimental import pallas as pl
from jax.experimental.pallas import tpu as pltpu
from jax.sharding import PartitionSpec as P

LANES = 128
CHUNK = 8
HEAD = 16
TAIL = 8
PATTERN = jnp.bfloat16
LEVELS = 65000.0
VMEM_BYTES = 40 * 1024 * 1024
HBM = pl.BlockSpec(memory_space=pltpu.HBM)
SMEM = pl.BlockSpec(memory_space=pltpu.SMEM)
VMEM = pl.BlockSpec(memory_space=pltpu.VMEM)


def call(kernel, name, out_shape, flops=0, moved=0, **more):
    return pl.pallas_call(
        kernel,
        out_shape=out_shape,
        name=name,
        compiler_params=pltpu.CompilerParams(vmem_limit_bytes=VMEM_BYTES),
        cost_estimate=pl.CostEstimate(flops=flops, bytes_accessed=moved, transcendentals=0),
        **more,
    )


def fetch(pairs, sems):
    copies = [pltpu.make_async_copy(source, place, sems.at[i]) for i, (source, place) in enumerate(pairs)]
    for c in copies:
        c.start()
    return copies


def pack_kernel(bins_hbm, rad_hbm, out_ref, bins_ref, rad_ref, sems):
    for c in fetch([(bins_hbm, bins_ref), (rad_hbm, rad_ref)], sems):
        c.wait()
    bins = bins_ref[:]
    kbins = bins.shape[0]
    fill = jnp.zeros((HEAD - 3 * kbins, bins.shape[1]), jnp.float32)
    parts = [rad_ref[:].astype(jnp.float32), (bins // LANES).astype(jnp.float32), (bins % LANES).astype(jnp.float32)]
    head = jnp.concatenate(parts + [fill], axis=0).astype(jnp.bfloat16)
    for g in range(out_ref.shape[0]):
        out_ref[g] = head


def sums_kernel(zones):
    def kernel(zone_hbm, area_hbm, openness_hbm, out_ref, zone_ref, area_ref, openness_ref, sems):
        for c in fetch([(zone_hbm, zone_ref), (area_hbm, area_ref), (openness_hbm, openness_ref)], sems):
            c.wait()
        zone, area = zone_ref[:], area_ref[:]
        lane = lax.broadcasted_iota(jnp.int32, (1, LANES), 1)
        values = [area * openness_ref[:], area, area * area]
        rows = [jnp.zeros((1, LANES), jnp.float32)] * len(values)
        for z in range(zones):
            member = zone == z
            for k, value in enumerate(values):
                rows[k] = jnp.where(lane == z, jnp.sum(jnp.where(member, value, 0.0), keepdims=True), rows[k])
        out_ref[:] = jnp.zeros_like(out_ref)
        for k, row in enumerate(rows):
            out_ref[k : k + 1] = row

    return kernel


def fetch_kernel(coef_hbm, tail_hbm, out_ref, sems):
    tail = tail_hbm.shape[0]
    whole = out_ref.shape[0] - tail
    pairs = [(coef_hbm.at[pl.ds(0, whole)], out_ref.at[pl.ds(0, whole)]), (tail_hbm, out_ref.at[pl.ds(whole, tail)])]
    for c in fetch(pairs, sems):
        c.wait()


def sun_kernel(groups, kbins):
    def kernel(heads, coef_ref, out_ref, acc, pattern, block):
        rows = heads.shape[2]
        lane = lax.broadcasted_iota(jnp.int32, (rows, LANES), 1)
        for g in range(groups):
            small = heads[g].astype(jnp.float32).T
            value = jnp.zeros((rows, LANES), jnp.float32)
            where = jnp.zeros((rows, LANES), jnp.float32)
            for k in range(kbins):
                low = small[:, 2 * kbins + k : 2 * kbins + k + 1].astype(jnp.int32)
                hit = lane == low
                value = jnp.where(hit, small[:, k : k + 1], value)
                where = jnp.where(hit, small[:, kbins + k : kbins + k + 1], where)
            pattern[g * rows : (g + 1) * rows] = value.astype(pattern.dtype)
            block[g * rows : (g + 1) * rows] = where.astype(block.dtype)

        blocks = coef_ref.shape[0] // LANES
        for first in range(0, blocks, CHUNK):
            count = min(CHUNK, blocks - first)
            parts = []
            for c in range(first, first + count):
                here = block[:] == jnp.asarray(c, block.dtype)
                parts.append(jnp.where(here, pattern[:], jnp.zeros_like(pattern)).astype(jnp.bfloat16))
            weights = jnp.concatenate(parts, axis=1) if count > 1 else parts[0]
            rows_at = slice(first * LANES, (first + count) * LANES)
            part = jnp.dot(weights, coef_ref[rows_at], preferred_element_type=jnp.float32)
            acc[:] = part if first == 0 else acc[:] + part

        for g in range(groups):
            sun = acc[g * rows : (g + 1) * rows]
            power = jnp.ceil(jnp.log2(jnp.maximum(jnp.max(sun, axis=0, keepdims=True), 1e-30)))
            code = jnp.round(sun * (LEVELS / jnp.exp2(power)) - 0.5 * LEVELS)
            out_ref[g, :rows] = code.astype(jnp.int32).astype(jnp.int16)
            power = jnp.broadcast_to(power, (TAIL, power.shape[1]))
            out_ref[g, rows:] = power.astype(jnp.int32).astype(jnp.int16)

    return kernel


def base_kernel(sky_ref, open_ref, closed_ref, cross_ref, closed_out):
    over = (((0,), (0,)), ((), ()))
    closed = lax.dot_general(sky_ref[:], closed_ref[:], over, preferred_element_type=jnp.float32)
    opened = lax.dot_general(sky_ref[:], open_ref[:], over, preferred_element_type=jnp.float32)
    closed_out[:] = closed
    cross_ref[:] = opened - closed


def own_sums(place_ref, sums_ref):
    sums = jnp.sum(sums_ref[:], axis=0)
    lane = lax.broadcasted_iota(jnp.int32, (1, LANES), 1)
    own = lane == place_ref[0]
    return [jnp.sum(jnp.where(own, sums[k : k + 1], 0.0), keepdims=True) for k in range(2)]


def cross_of(codes, base_ref, g):
    rows, width = base_ref.shape[0], codes.shape[2]
    scale = jnp.exp2(codes[g, rows:].astype(jnp.int32).astype(jnp.float32)[:1]) / LEVELS
    sun = (codes[g, :rows].astype(jnp.int32).astype(jnp.float32) + 0.5 * LEVELS) * scale
    return base_ref[:, g * width : (g + 1) * width] + sun


def grad_kernel(place_ref, sums_ref, codes, base_ref, closed_ref, target_ref, out_ref):
    num, den = own_sums(place_ref, sums_ref)
    share = num / den
    rows, width = base_ref.shape[0], codes.shape[2]
    total = jnp.zeros((8, width), jnp.float32)
    for g in range(codes.shape[0]):
        at = slice(g * width, (g + 1) * width)
        cross = cross_of(codes, base_ref, g)
        lit = closed_ref[:, at] + share * cross
        term = (lit - target_ref[:, at].astype(jnp.float32)) * cross
        total = total + jnp.sum(term.reshape(rows // 8, 8, width), axis=0)
    out_ref[:] = jnp.broadcast_to((2.0 * jnp.sum(total, keepdims=True))[None], out_ref.shape)


def lit_kernel(place_ref, sums_ref, codes, base_ref, closed_ref, out_ref):
    num, den = own_sums(place_ref, sums_ref)
    share = num / den
    width = codes.shape[2]
    for g in range(codes.shape[0]):
        at = slice(g * width, (g + 1) * width)
        out_ref[:, at] = (closed_ref[:, at] + share * cross_of(codes, base_ref, g)).astype(jnp.bfloat16)


def step_kernel(groups, zones, windows):
    def kernel(heard_ref, sums_ref, zone_hbm, area_hbm, openness_hbm, out_ref, zone_ref, area_ref, openness_ref, sems):
        copies = fetch([(zone_hbm, zone_ref), (area_hbm, area_ref), (openness_hbm, openness_ref)], sems)
        sums = jnp.sum(sums_ref[:], axis=0)
        ratios = []
        square = jnp.zeros((1, 1), jnp.float32)
        for z in range(zones):
            grads = jnp.sum(heard_ref[z * groups : (z + 1) * groups], axis=0)[:, 0:1]
            ratios.append(grads / sums[1:2, z : z + 1])
            square = square + ratios[z] * ratios[z] * sums[2:3, z : z + 1]
        rms = jnp.sqrt(square / windows + 1e-06)
        for c in copies:
            c.wait()
        zone = zone_ref[:]
        chosen = jnp.zeros(zone.shape, jnp.float32)
        for z in range(zones):
            chosen = jnp.where(zone == z, ratios[z], chosen)
        out_ref[:] = jnp.clip(openness_ref[:] - 0.25 * (area_ref[:] * chosen) / rms, 0.0, 1.0)

    return kernel


def local(sky, sky_open, sky_closed, sun_coef, sun_bins, sun_rad, target, zone_of, area, openness):
    zones = lax.axis_size("sens")
    groups = lax.axis_size("hour")
    own_zone = lax.axis_index("sens").astype(jnp.int32)[None]
    rows, patches = sky.shape
    kbins = sun_bins.shape[1]
    nbins, width = sun_coef.shape
    hours = rows * groups
    windows = area.shape[0]
    assert nbins % LANES == 0 or nbins % LANES >= 2 * kbins
    assert nbins <= 256 * LANES and width % LANES == 0 and windows % LANES == 0 and 3 * kbins <= HEAD
    assert zones <= LANES and rows % 16 == 0
    shape = jax.ShapeDtypeStruct
    f32, bf16 = jnp.float32, jnp.bfloat16
    dma = lambda n: pltpu.SemaphoreType.DMA((n,))

    packed = call(
        pack_kernel,
        "pack",
        shape((groups, HEAD, rows), bf16),
        in_specs=[HBM, HBM],
        scratch_shapes=[pltpu.VMEM((kbins, rows), jnp.int32), pltpu.VMEM((kbins, rows), bf16), dma(2)],
    )(sun_bins.T, sun_rad.T)
    heads = lax.all_to_all(packed, "hour", 0, 0)

    tiles = (windows // LANES, LANES)
    zone2, area2, openness2 = zone_of.reshape(tiles), area.reshape(tiles), openness.reshape(tiles)
    own_windows = [pltpu.VMEM(tiles, jnp.int32), pltpu.VMEM(tiles, f32), pltpu.VMEM(tiles, f32), dma(3)]
    zone_sums = call(
        sums_kernel(zones), "sums", shape((8, LANES), f32), in_specs=[HBM] * 3, scratch_shapes=own_windows
    )(zone2, area2, openness2)
    sums = lax.all_gather(zone_sums, "sens", axis=0)

    blocks = pl.cdiv(nbins, LANES)
    tail = jnp.pad(sun_coef[(blocks - 1) * LANES :], ((0, blocks * LANES - nbins), (0, 0)))
    coef = call(
        fetch_kernel,
        "coefficients",
        shape((blocks * LANES, width), bf16),
        moved=4 * nbins * width,
        in_specs=[HBM, HBM],
        out_specs=VMEM,
        scratch_shapes=[dma(2)],
    )(sun_coef, tail)

    codes = call(
        sun_kernel(groups, kbins),
        "sun",
        shape((groups, rows + TAIL, width), jnp.int16),
        flops=2 * hours * nbins * width,
        moved=2 * nbins * width,
        in_specs=[VMEM, VMEM],
        scratch_shapes=[
            pltpu.VMEM((hours, width), f32),
            pltpu.VMEM((hours, LANES), PATTERN),
            pltpu.VMEM((hours, LANES), PATTERN),
        ],
    )(heads, coef)
    codes = lax.all_to_all(codes, "hour", 0, 0)

    base, closed = call(
        base_kernel,
        "base",
        [shape((rows, groups * width), f32)] * 2,
        flops=4 * rows * patches * groups * width,
        moved=8 * rows * groups * width,
    )(sky.T, sky_open, sky_closed)
    message = call(
        grad_kernel,
        "grad",
        shape((zones * groups, 1, LANES), f32),
        in_specs=[SMEM] + [VMEM] * 5,
        flops=8 * hours * width,
        moved=12 * hours * width,
    )(own_zone, sums, codes, base, closed, target)
    heard = lax.all_to_all(message, ("sens", "hour"), 0, 0)
    illuminance = call(
        lit_kernel,
        "lit",
        shape((rows, groups * width), bf16),
        in_specs=[SMEM] + [VMEM] * 4,
        flops=4 * hours * width,
        moved=12 * hours * width,
    )(own_zone, sums, codes, base, closed)
    new_openness = call(
        step_kernel(groups, zones, windows * zones),
        "step",
        shape(tiles, f32),
        in_specs=[VMEM, VMEM] + [HBM] * 3,
        scratch_shapes=own_windows,
    )(heard, sums, zone2, area2, openness2)
    return (illuminance, new_openness.reshape(-1))


def solution(mesh):
    in_specs = (
        P("hour", None),
        P(None, "sens"),
        P(None, "sens"),
        P(None, ("sens", "hour")),
        P("hour", None),
        P("hour", None),
        P("hour", "sens"),
        P("sens", None),
        P("sens"),
        P("sens"),
    )
    out_specs = (P("hour", "sens"), P("sens"))
    return jax.shard_map(local, mesh=mesh, in_specs=in_specs, out_specs=out_specs, check_vma=False)
```

time: 431 us -> 57 us (0.13)
  waiting for transfers between devices: 346 us -> 9.73 us
  blocking collectives: 49.2 us -> 9.08 us
  between operations: 17.5 us -> 0.72 us
  starting transfers between devices: 0.04 us -> 15.1 us
  matrix products: 14.5 us -> 0 us
  Pallas kernels: 0 us -> 10.1 us
  local copies, waits for them, and re-layouts: 2.12 us -> 11.7 us
    all_gather x1 -> x0, waiting for transfers between devices: 346 us -> none  [local(): lax.all_gather(sun_coef, 'hour', axis=1, tiled=True)]
    psum x3 -> x0, blocking collectives: 37.1 us -> none  [the longest x1 15.1 us: local(): totals = lax.psum(partial_sums, 'sens')]
    all_to_all x0 -> x3, starting transfers between devices: none -> 15.1 us  [the longest x1 6.33 us: local(): heads = lax.all_to_all(packed, 'hour', 0, 0)]
    dot_general x5 -> x0, matrix products: 14.5 us -> none  [the longest x1 11 us: local(): jnp.dot(weights, lax.all_gather(sun_coef, 'hour', axis=1, tiled=True), pr...]
    unnamed x1 -> x0, blocking collectives: 12 us -> none
    pallas_call x0 -> x8, Pallas kernels: none -> 10.1 us  [the longest x1 4.88 us: local(): call(sun_kernel(groups, kbins), 'sun', shape((groups, rows + TAIL, width)...]
    all_to_all x0 -> x3, waiting for transfers between devices: none -> 9.73 us  [the longest x1 5.93 us: local(): heard = lax.all_to_all(message, ('sens', 'hour'), 0, 0)]
    unnamed x23 -> x24, local copies, waits for them, and re-layouts: 1.52 us -> 10.9 us
  transfers between devices with their start and end apart: 1 -> 3, of which waited for: 1 -> 2; matrix products, arithmetic and copies ran while one was open for 1% -> 1% of each run, Pallas kernels for 0% -> 4%
where the time goes in v2:
time: 57 us; the launch traced here: 56.4 us
  starting transfers between devices  15.1 us (26%)
  local copies, waits for them, and re-layouts  11.7 us (21%)
  Pallas kernels  10.1 us (18%)
  waiting for transfers between devices  9.73 us (17%)
  blocking collectives  9.08 us (16%)
  between operations  0.72 us (1%)
    unnamed x24, local copies, waits for them, and re-layouts  10.9 us
    all_gather x1, blocking collectives, local(): sums = lax.all_gather(zone_sums, 'sens', axis=0)  9.08 us
    all_to_all x1, starting transfers between devices, local(): heads = lax.all_to_all(packed, 'hour', 0, 0)  6.33 us
    all_to_all x1, waiting for transfers between devices, local(): heard = lax.all_to_all(message, ('sens', 'hour'), 0, 0)  5.93 us
    all_to_all x1, starting transfers between devices, local(): codes = lax.all_to_all(codes, 'hour', 0, 0)  5.1 us
    pallas_call x1, Pallas kernels, local(): call(sun_kernel(groups, kbins), 'sun', shape((groups, rows + TAIL, width)...  4.88 us
    all_to_all x1, waiting for transfers between devices, local(): codes = lax.all_to_all(codes, 'hour', 0, 0)  3.8 us
    all_to_all x1, starting transfers between devices, local(): heard = lax.all_to_all(message, ('sens', 'hour'), 0, 0)  3.71 us
  transfers between devices with their start and end apart: 3, of which 2 were waited for; matrix products, arithmetic and copies ran while one was open for 1% of the time, Pallas kernels for 4%

profile of v2, /device:TPU:0, one launch (start us, length us, event | category | flops | bytes accessed | tf_op | source)
XLA Modules:
  0.0 56.4 jit_solution(15770926277973361108)
XLA Ops:
  0.6 0.7 %copy-done.10 = s32[128,4]{0,1:T(4,128)S(1)} copy-done((s32[128,4]{0,1:T(4,128)S(1)}, s32[128,4]{0,1:T(4,128)}, u32[]{:S(2)}) %copy-start.10) | copy-done | bytes 2072
  1.3 0.7 %copy-done.11 = bf16[128,4]{0,1:T(4,128)(2,1)S(1)} copy-done((bf16[128,4]{0,1:T(4,128)(2,1)S(1)}, bf16[128,4]{0,1:T(4,128)(2,1)}, u32[]{:S(2)}) %copy-start.11) | copy-done | bytes 1048
  2.0 0.6 %pack.1 = bf16[4,16,128]{2,1,0:T(8,128)(2,1)} custom-call(s32[4,128]{1,0:T(4,128)S(1)} %bitcast.19, bf16[4,128]{1,0:T(4,128)(2,1)S(1)} %bitcast.20), custom_call_target="tpu_custom_call" | custom-call | tf_op jit(solution)/shard_map/pack/pallas_call | solution.py:199
  2.6 6.3 %all-to-all-start = ((bf16[4,16,128]{2,1,0:T(8,128)(2,1)}), bf16[4,16,128]{2,1,0:T(8,128)(2,1)S(1)}, u32[]{:S(2)}, u32[]{:S(2)}) async-start(bf16[4,16,128]{2,1,0:T(8,128)(2,1)} %pack.1), calls=%async_computation | async-start | bytes 32768 | tf_op jit(solution)/shard_map/all_to_all | solution.py:206
  9.0 0.8 %slice.3 = bf16[45,512]{1,0:T(8,128)(2,1)S(1)} slice(bf16[5165,512]{1,0:T(8,128)(2,1)} %coef_hbm.1), slice={[5120:5165], [0:512]} | slice | bytes 92160 | tf_op jit(solution)/shard_map/slice | solution.py:217
  9.8 0.0 copy-start
  9.8 2.5 %copy-done = bf16[5165,512]{1,0:T(8,128)(2,1)S(1)} copy-done((bf16[5165,512]{1,0:T(8,128)(2,1)S(1)}, bf16[5165,512]{1,0:T(8,128)(2,1)}, u32[]{:S(2)}) %copy-start) | copy-done | bytes 5288984
  12.3 0.5 coefficients.1.coef_ref
  12.8 2.4 %copy-done.1 = bf16[5248,512]{1,0:T(8,128)(2,1)} copy-done((bf16[5248,512]{1,0:T(8,128)(2,1)}, bf16[5248,512]{1,0:T(8,128)(2,1)S(1)}, u32[]{:S(2)}) %copy-start.1) | copy-done | bytes 5373976
  15.2 2.5 %copy-done.2 = bf16[5248,512]{1,0:T(8,128)(2,1)S(1)} copy-done((bf16[5248,512]{1,0:T(8,128)(2,1)S(1)}, bf16[5248,512]{1,0:T(8,128)(2,1)}, u32[]{:S(2)}) %copy-start.2) | copy-done | bytes 5373976
  17.8 0.0 copy-start.6
  17.8 4.9 %sun.1 = s16[4,136,512]{2,1,0:T(8,128)(2,1)} custom-call(bf16[4,16,128]{2,1,0:T(8,128)(2,1)S(1)} %all-to-all-done.heads, bf16[5248,512]{1,0:T(8,128)(2,1)S(1)} %copy-done.2), custom_call_target="tpu_custom_call" | custom-call | flops 2707947520 | bytes 5288960 | tf_op jit(solution)/shard_map/sun/pallas_call | solution.py:228
  22.7 5.1 %all-to-all-start.1 = ((s16[4,136,512]{2,1,0:T(8,128)(2,1)}), s16[4,136,512]{2,1,0:T(8,128)(2,1)S(1)}, u32[]{:S(2)}, u32[]{:S(2)}) async-start(s16[4,136,512]{2,1,0:T(8,128)(2,1)} %sun.1), calls=%async_computation.1 | async-start | bytes 1114112 | tf_op jit(solution)/shard_map/all_to_all | solution.py:241
  27.8 0.2 sums.1
  28.0 9.1 %all-gather = f32[64,128]{1,0:T(8,128)S(1)} all-gather(f32[8,128]{1,0:T(8,128)S(1)} %sums.1), channel_id=2, replica_groups=mesh['sens'=8,'hour'=4] {'sens'}, dimensions={0}, use_global_device_ids=true | all-gather | bytes 36864 | tf_op jit(solution)/shard_map/all_gather | solution.py:214
  37.0 1.1 %copy-done.4 = bf16[146,2048]{1,0:T(8,128)(2,1)S(1)} copy-done((bf16[146,2048]{1,0:T(8,128)(2,1)S(1)}, bf16[146,2048]{1,0:T(8,128)(2,1)}, u32[]{:S(2)}) %copy-start.4) | copy-done | bytes 598040
  38.1 0.5 base.1
  38.6 3.8 %all-to-all-done.1.codes = s16[4,136,512]{2,1,0:T(8,128)(2,1)S(1)} async-done(((s16[4,136,512]{2,1,0:T(8,128)(2,1)}), s16[4,136,512]{2,1,0:T(8,128)(2,1)S(1)}, u32[]{:S(2)}, u32[]{:S(2)}) %all-to-all-start.1) | async-done | bytes 557088 | tf_op jit(solution)/shard_map/all_to_all | solution.py:241
  42.4 1.0 %copy-done.5 = bf16[128,2048]{1,0:T(8,128)(2,1)S(1)} copy-done((bf16[128,2048]{1,0:T(8,128)(2,1)S(1)}, bf16[128,2048]{1,0:T(8,128)(2,1)}, u32[]{:S(2)}) %copy-start.5) | copy-done | bytes 524312
  43.4 1.3 %grad.1 = f32[32,1,128]{2,1,0:T(1,128)} custom-call(s32[1]{0:T(128)} %bitcast.place_ref, f32[8,8,128]{2,1,0:T(8,128)S(1)} %bitcast.9, s16[4,136,512]{2,1,0:T(8,128)(2,1)S(1)} %all-to-all-done.1.codes, f32[128,2048]{1,0:T(8,128)S(1)} %get-tuple-element.4.base_ref, f32[128,2048]{1,0:T(8,128)S(1)} %get-tuple-element.5.closed_ref, bf16[128,2048]{1,0:T(8,128)(2,1)S(1)} %copy-done.5), custom_call_target="tpu_custom_call" | custom-call | flops 2097152 | bytes 3145728 | tf_op jit(solution)/shard_map/grad/pallas_call | solution.py:250
  44.8 3.7 %all-to-all-start.2 = ((f32[32,1,128]{2,1,0:T(1,128)}), f32[32,1,128]{2,1,0:T(1,128)S(1)}, u32[]{:S(2)}, u32[]{:S(2)}) async-start(f32[32,1,128]{2,1,0:T(1,128)} %grad.1), calls=%async_computation.2 | async-start | bytes 32768 | tf_op jit(solution)/shard_map/all_to_all | solution.py:258
  48.5 1.2 %lit.1 = bf16[128,2048]{1,0:T(8,128)(2,1)} custom-call(s32[1]{0:T(128)} %bitcast.place_ref, f32[8,8,128]{2,1,0:T(8,128)S(1)} %bitcast.10, s16[4,136,512]{2,1,0:T(8,128)(2,1)S(1)} %all-to-all-done.1.codes, f32[128,2048]{1,0:T(8,128)S(1)} %get-tuple-element.4.base_ref, f32[128,2048]{1,0:T(8,128)S(1)} %get-tuple-element.5.closed_ref), custom_call_target="tpu_custom_call" | custom-call | flops 1048576 | bytes 3145728 | tf_op jit(solution)/shard_map/lit/pallas_call | solution.py:259
  49.7 5.9 %all-to-all-done.2.heard_ref = f32[32,1,128]{2,1,0:T(1,128)S(1)} async-done(((f32[32,1,128]{2,1,0:T(1,128)}), f32[32,1,128]{2,1,0:T(1,128)S(1)}, u32[]{:S(2)}, u32[]{:S(2)}) %all-to-all-start.2) | async-done | bytes 16416 | tf_op jit(solution)/shard_map/all_to_all | solution.py:258
  55.6 0.8 %step.1 = f32[8,128]{1,0:T(8,128)} custom-call(f32[32,1,128]{2,1,0:T(1,128)S(1)} %all-to-all-done.2.heard_ref, f32[8,8,128]{2,1,0:T(8,128)S(1)} %bitcast.11, s32[8,128]{1,0:T(8,128)S(1)} %bitcast.14, f32[8,128]{1,0:T(8,128)S(1)} %bitcast.16, f32[8,128]{1,0:T(8,128)S(1)} %bitcast.18), custom_call_target="tpu_custom_call" | custom-call | tf_op jit(solution)/shard_map/step/pallas_call | solution.py:267
  (17 shorter events, 0.0 us)
Async XLA Ops:
  0.6 0.7 %copy-start.10 = (s32[128,4]{0,1:T(4,128)S(1)}, s32[128,4]{0,1:T(4,128)}, u32[]{:S(2)}) copy-start(s32[128,4]{0,1:T(4,128)} %param.14) | copy-start | bytes 6148
  1.3 0.7 %copy-start.11 = (bf16[128,4]{0,1:T(4,128)(2,1)S(1)}, bf16[128,4]{0,1:T(4,128)(2,1)}, u32[]{:S(2)}) copy-start(bf16[128,4]{0,1:T(4,128)(2,1)} %param.15) | copy-start | bytes 3076
  2.6 12.6 %all-to-all-start = ((bf16[4,16,128]{2,1,0:T(8,128)(2,1)}), bf16[4,16,128]{2,1,0:T(8,128)(2,1)S(1)}, u32[]{:S(2)}, u32[]{:S(2)}) async-start(bf16[4,16,128]{2,1,0:T(8,128)(2,1)} %pack.1), calls=%async_computation | async-start | bytes 32768 | tf_op jit(solution)/shard_map/all_to_all | solution.py:206
  9.8 2.5 %copy-start = (bf16[5165,512]{1,0:T(8,128)(2,1)S(1)}, bf16[5165,512]{1,0:T(8,128)(2,1)}, u32[]{:S(2)}) copy-start(bf16[5165,512]{1,0:T(8,128)(2,1)} %coef_hbm.1) | copy-start | bytes 15866884
  12.8 2.4 %copy-start.1 = (bf16[5248,512]{1,0:T(8,128)(2,1)}, bf16[5248,512]{1,0:T(8,128)(2,1)S(1)}, u32[]{:S(2)}) copy-start(bf16[5248,512]{1,0:T(8,128)(2,1)S(1)} %coefficients.1.coef_ref) | copy-start | bytes 16121860
  15.2 2.5 %copy-start.2 = (bf16[5248,512]{1,0:T(8,128)(2,1)S(1)}, bf16[5248,512]{1,0:T(8,128)(2,1)}, u32[]{:S(2)}) copy-start(bf16[5248,512]{1,0:T(8,128)(2,1)} %copy-done.1) | copy-start | bytes 16121860
  17.7 10.0 %copy-start.7 = (s32[1024,1]{0,1:T(1,128)S(1)}, s32[1024,1]{0,1:T(1,128)}, u32[]{:S(2)}) copy-start(s32[1024,1]{0,1:T(1,128)} %param.17) | copy-start | bytes 12292
  17.8 10.0 %copy-start.8 = (f32[1024]{0:T(1024)S(1)}, f32[1024]{0:T(1024)}, u32[]{:S(2)}) copy-start(f32[1024]{0:T(1024)} %param.18) | copy-start | bytes 12292
  17.8 10.0 %copy-start.9 = (f32[1024]{0:T(1024)S(1)}, f32[1024]{0:T(1024)}, u32[]{:S(2)}) copy-start(f32[1024]{0:T(1024)} %param.19) | copy-start | bytes 12292
  17.8 19.3 %copy-start.3 = (bf16[146,2048]{1,0:T(8,128)(2,1)S(1)}, bf16[146,2048]{1,0:T(8,128)(2,1)}, u32[]{:S(2)}) copy-start(bf16[146,2048]{1,0:T(8,128)(2,1)} %open_ref.1) | copy-start | bytes 1794052
  17.8 19.3 %copy-start.6 = (bf16[128,146]{0,1:T(8,128)(2,1)S(1)}, bf16[128,146]{0,1:T(8,128)(2,1)}, u32[]{:S(2)}) copy-start(bf16[128,146]{0,1:T(8,128)(2,1)} %param.10) | copy-start | bytes 112132
  22.7 19.7 %all-to-all-start.1 = ((s16[4,136,512]{2,1,0:T(8,128)(2,1)}), s16[4,136,512]{2,1,0:T(8,128)(2,1)S(1)}, u32[]{:S(2)}, u32[]{:S(2)}) async-start(s16[4,136,512]{2,1,0:T(8,128)(2,1)} %sun.1), calls=%async_computation.1 | async-start | bytes 1114112 | tf_op jit(solution)/shard_map/all_to_all | solution.py:241
  37.0 1.1 %copy-start.4 = (bf16[146,2048]{1,0:T(8,128)(2,1)S(1)}, bf16[146,2048]{1,0:T(8,128)(2,1)}, u32[]{:S(2)}) copy-start(bf16[146,2048]{1,0:T(8,128)(2,1)} %closed_ref.1) | copy-start | bytes 1794052
  42.4 1.0 %copy-start.5 = (bf16[128,2048]{1,0:T(8,128)(2,1)S(1)}, bf16[128,2048]{1,0:T(8,128)(2,1)}, u32[]{:S(2)}) copy-start(bf16[128,2048]{1,0:T(8,128)(2,1)} %target_ref.1) | copy-start | bytes 1572868
  44.8 10.9 %all-to-all-start.2 = ((f32[32,1,128]{2,1,0:T(1,128)}), f32[32,1,128]{2,1,0:T(1,128)S(1)}, u32[]{:S(2)}, u32[]{:S(2)}) async-start(f32[32,1,128]{2,1,0:T(1,128)} %grad.1), calls=%async_computation.2 | async-start | bytes 32768 | tf_op jit(solution)/shard_map/all_to_all | solution.py:258
